TPU v7x, 128 devices: a whole 4x4x4 slice. The times are simulated.
128 devices in a mesh: sub: 4 (over x), row: 4 (over z), col: 8 (over y, core).
Axes of the slice: x: 4, y: 4, z: 4, core: 2. Of those that a mesh axis runs over, the one named last changes fastest.
Arguments:
- parent_front: float32 [16384, 16384], P(('sub', 'row'), 'col')
- child_panel: float32 [4, 8192, 512], P('sub', 'row'), may hold values from -0.25 to 0.25
- child_pattern: int32 [4, 64, 4], P('sub', 'row'), may hold values 0 or 1
- child_map: int32 [4, 64], replicated, may hold values from 0 to 127, as said below
Outputs:
- schur_block: float32 [16384, 16384], P(('sub', 'row'), 'col')
- panel_factor: float32 [16384, 512], P(('sub', 'row'))
Inputs may be any that keep to these rules, and one draw needn't show every extreme that they name: `child_map`: within a child the values are distinct. Child block i, with r = i // (2 * 8), c = (i // 2) % 8 and e = i % 2, maps into parent blocks c * 16 to (c + 1) * 16 - 1, and within one child and one c the value rises with e * 4 + r. Hence at most 2 of the blocks i with one r and one c fall in one row group of 8 parent blocks; in every draw some row group receives exactly 2 such blocks from every r and every child.
All inputs are finite; a program needn't handle non-finite values. No bound on the sum of `child_pattern` on one device may be relied on, other than what follows from the above.
Results may differ from a plain program's by a relative error of at most 0.0001.
Values sent between devices are 32-bit elements; how exact they have to be, the bound alone decides.
No kernel may reach another device: no remote copies, remote signals or barrier semaphores. Data moves between devices by JAX's collectives and lax.ppermute only.
A program may use at most 128 MiB of HBM per device.

v0:
```python
import jax
import jax.numpy as jnp
from jax import lax
from jax.sharding import PartitionSpec as P

B = 128
K = 512
E = 2
PW = 4


def broadcast(x, axis, root):
    mine = lax.axis_index(axis) == root
    return lax.psum(jnp.where(mine, x, jnp.zeros_like(x)), axis)


def from_group(own_rows, root_group):
    return broadcast(own_rows, ("sub", "row"), root_group)


def per_device(parent_front, child_panel, child_pattern, child_map):
    sub_count = lax.axis_size("sub")
    row_count = lax.axis_size("row")
    col_count = lax.axis_size("col")
    groups = sub_count * row_count
    group_span = groups // col_count
    sub_index = lax.axis_index("sub")
    row_index = lax.axis_index("row")
    col_index = lax.axis_index("col")
    group = sub_index * row_count + row_index
    tile_rows = parent_front.shape[0]
    tile_cols = parent_front.shape[1]
    row_blocks = tile_rows // B
    col_blocks = tile_cols // B
    local_blocks = child_panel.shape[1] // B
    panel_blocks = K // B
    weights = child_pattern[0].astype(jnp.float32)
    masked = (
        child_panel[0].reshape(local_blocks, B, panel_blocks, B) * weights[:, None, :, None]
    ).reshape(local_blocks * B, K)
    selected = lax.dynamic_slice_in_dim(masked, col_index * (E * B), E * B, 0)
    columns = lax.all_gather(selected, "row", axis=0, tiled=True)
    update = lax.dot_general(
        masked,
        columns,
        (((1,), (1,)), ((), ())),
        precision=lax.Precision.HIGHEST,
        preferred_element_type=jnp.float32,
    )
    tile_width = update.shape[1]
    own_map = lax.dynamic_slice_in_dim(child_map, sub_index, 1, 0)[0]
    sent_map = lax.dynamic_slice_in_dim(own_map, row_index * local_blocks, local_blocks, 0).reshape(
        col_count, E
    )
    targets = jnp.arange(groups, dtype=jnp.int32)
    dest_map = jnp.repeat(sent_map, group_span, axis=0)
    live_slots = (dest_map // row_blocks == targets[:, None]).astype(jnp.float32)
    outgoing = (
        jnp.repeat(update.reshape(col_count, E, B, tile_width), group_span, axis=0)
        * live_slots[:, :, None, None]
    )
    arrived = lax.all_to_all(outgoing, ("sub", "row"), split_axis=0, concat_axis=0, tiled=True)
    src_child = targets // row_count
    src_row = targets % row_count
    slot_range = jnp.arange(E, dtype=jnp.int32)
    sent_index = src_row[:, None] * local_blocks + group // group_span * E + slot_range[None, :]
    row_parent = child_map[src_child[:, None], sent_index]
    row_slot = (row_parent - group * row_blocks).reshape(sub_count, row_count * E)
    row_valid = (row_slot >= 0) & (row_slot < row_blocks)
    row_slot = jnp.where(row_valid, row_slot, row_blocks)
    tile_index = (
        jnp.arange(row_count, dtype=jnp.int32)[:, None] * local_blocks
        + col_index * E
        + slot_range[None, :]
    ).reshape(-1)
    col_slot = child_map[:, tile_index] - col_index * col_blocks
    arrived = arrived.reshape(sub_count, row_count * E, B, row_count * E, B).transpose(
        0, 1, 3, 2, 4
    )
    summed = jnp.zeros((row_blocks, B, col_blocks, B), jnp.float32)
    summed = summed.at[row_slot[:, :, None], :, col_slot[:, None, :], :].add(arrived, mode="drop")
    assembled = parent_front - summed.reshape(tile_rows, tile_cols)
    panel_width = PW * B
    panel_cols = broadcast(assembled[:, :panel_width], "col", 0)
    corner = broadcast(panel_cols[:panel_width], ("sub", "row"), 0)
    factor_top = jnp.linalg.cholesky(corner)
    solved = jax.scipy.linalg.solve_triangular(factor_top, panel_cols.T, lower=True).T
    global_row = group * tile_rows + jnp.arange(tile_rows, dtype=jnp.int32)
    padded = jnp.pad(factor_top, ((0, tile_rows - panel_width), (0, 0)))
    own_factor = jnp.where(global_row[:, None] < panel_width, padded, solved)
    first_group = col_index * group_span
    far_rows = jnp.concatenate(
        [from_group(own_factor, first_group + offset) for offset in range(group_span)], axis=0
    )
    schur_block = assembled - lax.dot_general(
        own_factor,
        far_rows,
        (((1,), (1,)), ((), ())),
        precision=lax.Precision.HIGHEST,
        preferred_element_type=jnp.float32,
    )
    return (schur_block, own_factor)


def solution(mesh):
    placed = (P(("sub", "row"), "col"), P("sub", "row", None), P("sub", "row", None), P())
    return jax.shard_map(
        per_device,
        mesh=mesh,
        in_specs=placed,
        out_specs=(P(("sub", "row"), "col"), P(("sub", "row"), None)),
        check_vma=False,
    )
```

profile of v0, /device:TPU:0, one launch (start us, length us, event | category | flops | bytes accessed | tf_op | source)
XLA Modules:
  0.0 921.8 jit_solution(9741707794713052913)
XLA Ops:
  7.2 0.7 convert_bitcast_fusion
  8.6 2.5 copy.70
  11.1 2.1 dynamic-slice_multiply_fusion
  13.8 33.0 %all-gather.2.cloned.1.call-done = f32[1024,512]{1,0:T(8,128)} async-done(((f32[256,512]{1,0:T(8,128)}), f32[1024,512]{1,0:T(8,128)}) %all-gather.2.cloned.1.call-update) | async-done | bytes 2097168 | tf_op jit(solution)/shard_map/all_gather | solution.py:42
  46.8 17.9 %fusion.4 = f32[8,2,128,1024]{2,3,1,0:T(8,128)} fusion(f32[8,2,128,512]{3,2,1,0:T(8,128)} %bitcast.99, f32[1024,512]{1,0:T(8,128)} %all-gather.2.cloned.1.call-done, f32[8,2,512]{2,1,0:T(2,128)S(1)} %mul.80), kind=kOutput, calls=%fused_computation.12 | convolution fusion | flops 12885950464 | bytes 14712832 | tf_op jit(solution)/shard_map/dot_general | solution.py:43
  64.8 11.0 %bitcast_multiply_fusion = f32[16,2,128,1024]{2,3,1,0:T(8,128)} fusion(f32[16,2]{1,0:T(8,128)S(1)} %copy.44, f32[8,2,128,1024]{2,3,1,0:T(8,128)} %fusion.4), kind=kLoop, calls=%fused_computation.5 | loop fusion | flops 4194304 | bytes 25165952 | tf_op jit(solution)/shard_map/mul | solution.py:59
  75.8 5.6 all-to-all-start
  81.9 0.8 gather_fusion
  84.2 9.3 %copy.47 = f32[1024,2048]{0,1:T(8,128)} copy(f32[1024,2048]{1,0:T(8,128)} %param.4) | data formatting | bytes 16777216 | tf_op args[0]
  93.4 281.1 %all-to-all-done = f32[16,2,128,1024]{2,3,1,0:T(8,128)} async-done(((f32[16,2,128,1024]{2,3,1,0:T(8,128)}), f32[16,2,128,1024]{2,3,1,0:T(8,128)}, u32[]{:S(2)}, u32[]{:S(2)}) %all-to-all-start) | async-done | bytes 16777248 | tf_op jit(solution)/shard_map/all_to_all | solution.py:62
  374.5 17.5 %copy.45 = f32[256,128,128]{2,1,0:T(8,128)} copy(f32[256,128,128]{1,2,0:T(8,128)} %bitcast.10) | data formatting | bytes 33554432 | tf_op jit(solution)/shard_map/transpose | solution.py:77
  392.0 4.3 broadcast_in_dim.22
  396.3 50.6 %scatter_fusion = f32[8,128,16,128]{3,1,2,0:T(8,128)} fusion(f32[8,128,16,128]{3,1,2,0:T(8,128)} %broadcast_in_dim.22, s32[256]{0:T(256)S(1)} %reshape.295, f32[256,128,128]{2,1,0:T(8,128)} %copy.45), kind=kCustom, calls=%fused_computation.2 | custom fusion | flops 4194304 | bytes 50333696 | tf_op jit(solution)/shard_map/scatter-add | solution.py:81
  446.9 9.3 %copy.46 = f32[8,128,16,128]{1,0,3,2:T(8,128)} copy(f32[8,128,16,128]{3,1,2,0:T(8,128)} %scatter_fusion) | data formatting | bytes 16777216 | tf_op jit(solution)/shard_map/scatter-add | solution.py:81
  456.2 12.3 %bitcast_subtract_fusion = f32[1024,2048]{0,1:T(8,128)} fusion(f32[1024,2048]{0,1:T(8,128)} %copy.47, f32[256,8,8,128]{3,2,1,0:T(8,128)} %bitcast.96), kind=kLoop, calls=%fused_computation.6 | loop fusion | flops 2097152 | bytes 25165824 | tf_op jit(solution)/shard_map/sub | solution.py:82
  468.5 3.2 slice_select_fusion
  471.7 70.8 %all-reduce.7.cloned.1.call-done = f32[1024,512]{0,1:T(8,128)} async-done(((f32[1024,512]{0,1:T(8,128)}), f32[1024,512]{0,1:T(8,128)}) %all-reduce.7.cloned.1.call-update) | async-done | bytes 2097168 | tf_op jit(solution)/shard_map/psum | solution.py:14
  542.6 2.3 slice_select_fusion.1
  545.4 87.7 %all-reduce.9.cloned.1.call-done = f32[512,512]{0,1:T(8,128)} async-done(((f32[512,512]{0,1:T(8,128)}), f32[512,512]{0,1:T(8,128)}) %all-reduce.9.cloned.1.call-update) | async-done | bytes 1048592 | tf_op jit(solution)/shard_map/psum | solution.py:14
  633.1 1.6 copy.48
  635.0 11.7 %cholesky.103 = f32[128,128]{1,0:T(8,128)S(1)} custom-call(f32[128,128]{1,0:T(8,128)S(1)} %cholesky.263), custom_call_target="Cholesky" | custom-call | tf_op jit(solution)/shard_map/jit(cholesky)/cholesky | solution.py:86
  646.8 9.8 %custom-call.31 = f32[1,128,128]{1,2,0:T(8,128)S(1)} custom-call(f32[1,128,128]{2,1,0:T(8,128)S(1)} %get-tuple-element.43), custom_call_target="InvertDiagBlocksLowerTriangular" | custom-call | tf_op jit(solution)/shard_map/jit(cholesky)/cholesky | solution.py:86
  657.3 11.7 %cholesky.215 = f32[128,128]{1,0:T(8,128)S(1)} custom-call(f32[128,128]{1,0:T(8,128)S(1)} %cholesky.267), custom_call_target="Cholesky" | custom-call | tf_op jit(solution)/shard_map/jit(cholesky)/cholesky | solution.py:86
  669.5 9.9 %custom-call.32 = f32[1,128,128]{1,2,0:T(8,128)S(1)} custom-call(f32[1,128,128]{2,1,0:T(8,128)S(1)} %get-tuple-element.41), custom_call_target="InvertDiagBlocksLowerTriangular" | custom-call | tf_op jit(solution)/shard_map/jit(cholesky)/cholesky | solution.py:86
  680.4 11.7 %cholesky.236 = f32[128,128]{1,0:T(8,128)S(1)} custom-call(f32[128,128]{1,0:T(8,128)S(1)} %cholesky.272), custom_call_target="Cholesky" | custom-call | tf_op jit(solution)/shard_map/jit(cholesky)/cholesky | solution.py:86
  692.3 9.8 %custom-call.33 = f32[1,128,128]{1,2,0:T(8,128)S(1)} custom-call(f32[1,128,128]{2,1,0:T(8,128)S(1)} %get-tuple-element.39), custom_call_target="InvertDiagBlocksLowerTriangular" | custom-call | tf_op jit(solution)/shard_map/jit(cholesky)/cholesky | solution.py:86
  702.9 11.9 %cholesky.253 = f32[128,128]{1,0:T(8,128)S(1)} custom-call(f32[128,128]{1,0:T(8,128)S(1)} %convolution_subtract_fusion.4), custom_call_target="Cholesky" | custom-call | tf_op jit(solution)/shard_map/jit(cholesky)/cholesky | solution.py:86
  714.9 0.6 compare_reduce_fusion.2
  715.6 0.6 compare_reduce_fusion.3
  716.2 0.7 compare_reduce_fusion.1
  716.9 0.6 compare_reduce_fusion
  720.0 1.6 fusion.25
  721.6 11.5 %while.1 = (s32[]{:T(128)}, f32[512,512]{0,1:T(8,128)}, s32[4,2]{0,1:T(2,128)S(1)}, f32[4,128,128]{2,1,0:T(8,128)S(1)}, s32[]{:T(128)}) while((s32[]{:T(128)}, f32[512,512]{0,1:T(8,128)}, s32[4,2]{0,1:T(2,128)S(1)}, f32[4,128,128]{2,1,0:T(8,128)S(1)}, s32[]{:T(128)}) %tuple.33), condition=%wide.while_cond, body=%wide.while_body.sunk | while | flops 2 | bytes 393321 | solution.py:87
  722.2 2.2 dynamic-slice.8
  725.1 2.2 dynamic-slice.8
  728.0 2.2 dynamic-slice.8
  730.9 2.1 dynamic-slice.8
  733.1 39.3 %custom-call.34 = f32[4,128,128]{1,2,0:T(8,128)S(1)} custom-call(f32[4,128,128]{2,1,0:T(8,128)S(1)} %get-tuple-element.9), custom_call_target="InvertDiagBlocksLowerTriangular" | custom-call | tf_op jit(solution)/shard_map/jit(_solve_triangular)/triangular_solve | solution.py:87
  773.1 1.5 convolution_subtract_fusion.1
  774.6 0.6 fusion.39
  775.2 1.6 convolution_subtract_fusion
  777.5 2.1 fusion.18
  780.3 1.9 broadcast_select_fusion.1
  782.1 1.5 broadcast_select_fusion
  783.6 1.8 copy.59
  785.4 101.2 %all-reduce.11.cloned.1.call-done = (f32[1024,512]{0,1:T(8,128)}, f32[1024,512]{0,1:T(8,128)}) async-done(((f32[1024,512]{0,1:T(8,128)}, f32[1024,512]{0,1:T(8,128)}), (f32[1024,512]{0,1:T(8,128)}, f32[1024,512]{0,1:T(8,128)})) %all-reduce.11.cloned.1.call-update) | async-done | bytes 4194320 | tf_op jit(solution)/shard_map/psum | solution.py:14
  886.7 19.0 %fusion.6 = f32[1024,2048]{0,1:T(8,128)} fusion(f32[1024,2048]{0,1:T(8,128)} %bitcast_subtract_fusion, f32[1024,512]{0,1:T(8,128)S(1)} %get-tuple-element.33, f32[1024,512]{0,1:T(8,128)} %get-tuple-element.30, f32[1024,512]{0,1:T(8,128)} %get-tuple-element.31), kind=kOutput, calls=%fused_computation.14 | convolution fusion | flops 12888047616 | bytes 23068672 | tf_op jit(solution)/shard_map/dot_general | solution.py:95
  905.7 9.1 copy.58
  (97 shorter events, 12.0 us)
Async XLA Ops:
  7.2 39.7 %all-gather.2.cloned.1.call-start = ((), (), s32[]{:S(2)}) async-start(), calls=%async_computation.1 | async-start | bytes 2621440 | tf_op jit(solution)/shard_map/all_gather | solution.py:42
  11.1 2.1 copy-start
  75.8 298.8 %all-to-all-start = ((f32[16,2,128,1024]{2,3,1,0:T(8,128)}), f32[16,2,128,1024]{2,3,1,0:T(8,128)}, u32[]{:S(2)}, u32[]{:S(2)}) async-start(f32[16,2,128,1024]{2,3,1,0:T(8,128)} %bitcast_multiply_fusion), calls=%async_computation | async-start | bytes 33554432 | tf_op jit(solution)/shard_map/all_to_all | solution.py:62
  81.4 461.2 %all-reduce.7.cloned.1.call-start = ((), (), s32[]{:S(2)}) async-start(), calls=%async_computation.2 | async-start | bytes 4194304 | tf_op jit(solution)/shard_map/psum | solution.py:14
  471.7 161.4 %all-reduce.9.cloned.1.call-start = ((), (), s32[]{:S(2)}) async-start(), calls=%async_computation.3 | async-start | bytes 2097152 | tf_op jit(solution)/shard_map/psum | solution.py:14
  544.9 341.8 %all-reduce.11.cloned.1.call-start = ((), (), s32[]{:S(2)}) async-start(), calls=%async_computation.4 | async-start | bytes 8388608 | tf_op jit(solution)/shard_map/psum | solution.py:14
  633.1 1.7 copy-start.2
  720.0 52.4 %copy-start.1 = (f32[1024,512]{0,1:T(8,128)S(1)}, f32[1024,512]{0,1:T(8,128)}, u32[]{:S(2)}) copy-start(f32[1024,512]{0,1:T(8,128)} %all-reduce.7.cloned.1.call-done) | copy-start | bytes 6291460
  777.5 2.8 copy-start.3
Sparse Core Ops, SparseCore 0:
  13.3 33.5 all-gather.1
  471.8 70.7 all-reduce.6
  546.4 86.6 all-reduce.8
  783.7 102.8 all-reduce.10
where the time goes:
time: 931 us; the launch traced here: 922 us
  waiting for transfers between devices  574 us (62%)
  other arithmetic  206 us (22%)
  local copies, waits for them, and re-layouts  70.9 us (8%)
  matrix products  47 us (5%)
  between operations  17.1 us (2%)
    all_to_all x1, waiting for transfers between devices, per_device(): lax.all_to_all(outgoing, ('sub', 'row'), split_axis=0, concat_axis=0, til...  281 us
    psum x3, waiting for transfers between devices, broadcast(): return lax.psum(jnp.where(mine, x, jnp.zeros_like(x)), axis)  260 us
    another operation x15, other arithmetic, per_device(): factor_top = jnp.linalg.cholesky(corner)  79.3 us
    scatter-add x1, other arithmetic, per_device(): summed.at[row_slot[:, :, None], :, col_slot[:, None, :], :]  50.6 us
    another operation x3, other arithmetic, per_device(): jax.scipy.linalg.solve_triangular(factor_top, panel_cols.T, lower=True)  40.9 us
    all_gather x1, waiting for transfers between devices, per_device(): columns = lax.all_gather(selected, 'row', axis=0, tiled=True)  33 us
    unnamed x13, local copies, waits for them, and re-layouts  22.8 us
    dot_general x1, matrix products, per_device(): lax.dot_general(own_factor, far_rows, (((1,), (1,)), ((), ())), precision...  19 us
  transfers between devices with their start and end apart: 5, of which 5 were waited for; matrix products, arithmetic and copies ran while one was open for 2% of the time, Pallas kernels for 0%

commit v1 on v0

v1 whole, which is shorter than its diff:
```python
import jax
import jax.numpy as jnp
from jax import lax
from jax.experimental import pallas as pl
from jax.experimental.pallas import tpu as pltpu
from jax.sharding import PartitionSpec as P

B = 128
K = 512
E = 2
PW = 512
ALL = ("sub", "row", "col")
NS, NR, NC = 4, 4, 8
OFFS = (0, 3, 1, 2)
F32 = jnp.float32
BF16 = jnp.bfloat16
MIB = 1 << 20


def gid(s, r, c):
    return (s * NR + r) * NC + c


DEVICES = [(s, r, c) for s in range(NS) for r in range(NR) for c in range(NC)]


def moved(axis, k, s, r, c):
    if axis == "x":
        return ((s + k) % NS, r, c)
    if axis == "z":
        return (s, (r + k) % NR, c)
    if axis == "y":
        return (s, r, (c + 2 * k) % NC)
    return (s, r, c ^ 1)


def axis_of(phase, c):
    return "zx"[(phase + c % 2) % 2]


def pairs(phase, k, where=lambda s, r, c: True):
    return [
        (gid(s, r, c), gid(*moved(axis_of(phase, c), k, s, r, c)))
        for s, r, c in DEVICES
        if where(s, r, c)
    ]


def move_pairs(axis, k, where=lambda s, r, c: True):
    return [(gid(s, r, c), gid(*moved(axis, k, s, r, c))) for s, r, c in DEVICES if where(s, r, c)]


def permute(x, prs):
    return lax.ppermute(x, ALL, prs)


def ring_phase(x, phase):
    half = x.shape[0] // 2
    up = permute(x, pairs(phase, 1))
    down = permute(x, pairs(phase, -1))
    far_a = permute(up[:half], pairs(phase, 1))
    far_b = permute(down[half:], pairs(phase, -1))
    return jnp.concatenate([x, up, down, far_a, far_b], axis=0)


def ring_gather(x):
    return ring_phase(ring_phase(x, 0), 1)


def split(x):
    hi = x.astype(BF16)
    lo = (x - hi.astype(F32)).astype(BF16)
    return hi, lo


def left_cat(x):
    hi, lo = split(x)
    return jnp.concatenate([hi, lo, hi], axis=1)


def right_cat(x):
    hi, lo = split(x)
    return jnp.concatenate([hi, hi, lo], axis=1)


def dot_t(a, b, precision=None):
    return lax.dot_general(
        a, b, (((1,), (1,)), ((), ())), precision=precision, preferred_element_type=F32
    )


def offset(p):
    return jnp.where(p == 0, 0, jnp.where(p == 1, 3, jnp.where(p == 2, 1, 2)))


def factor_block(rows):
    n = len(rows)
    w = list(rows)
    lane = lax.broadcasted_iota(jnp.int32, (8, B), 1)
    sub = lax.broadcasted_iota(jnp.int32, (8, B), 0)
    upper = [None] * n
    for j in range(0, B, 4):
        k0, o = j // 8, j % 8
        cols = [
            [jnp.broadcast_to(w[k][:, j + m : j + m + 1], (8, B)) for m in range(4)]
            for k in range(k0, n)
        ]
        top = cols[0]

        def elem(p, q):
            return jnp.broadcast_to(top[q][o + p : o + p + 1, :], (8, B))

        l = {}
        inv = [None] * 4
        for q in range(4):
            d = elem(q, q)
            for t in range(q):
                d = d - l[q, t] * l[q, t]
            y = lax.rsqrt(d)
            inv[q] = y * (1.5 - 0.5 * d * y * y)
            l[q, q] = d * inv[q]
            for p in range(q + 1, 4):
                e = elem(p, q)
                for t in range(q):
                    e = e - l[p, t] * l[q, t]
                l[p, q] = e * inv[q]
        in_block = (lane >= j) & (lane < j + 4)
        orig = [jnp.broadcast_to(w[k0][o + m : o + m + 1, :], (8, B)) for m in range(4)]
        ident = [
            jnp.where(in_block, jnp.where(lane == j + m, 1.0, 0.0).astype(F32), orig[m])
            for m in range(4)
        ]
        uo, ui = [], []
        for m in range(4):
            a, b = orig[m], ident[m]
            for t in range(m):
                a = a - l[m, t] * uo[t]
                b = b - l[m, t] * ui[t]
            uo.append(a * inv[m])
            ui.append(b * inv[m])
        back = [None] * 4
        for m in (3, 2, 1, 0):
            a = ui[m]
            for t in range(m + 1, 4):
                a = a - l[t, m] * back[t]
            back[m] = a * inv[m]
        acc_u = upper[k0] if upper[k0] is not None else jnp.zeros((8, B), F32)
        new_rows = w[k0]
        for m in range(4):
            at = sub == o + m
            acc_u = jnp.where(at & (lane >= j + m), uo[m], acc_u)
            new_rows = jnp.where(at, ui[m], new_rows)
        upper[k0] = acc_u
        for k in range(k0, n):
            if k == k0 and o == 4:
                w[k] = new_rows
                continue
            c = cols[k - k0]
            x = jnp.where(in_block, 0.0, w[k])
            x = x - (c[0] * back[0] + c[1] * back[1]) - (c[2] * back[2] + c[3] * back[3])
            w[k] = jnp.where(sub >= 4, x, new_rows) if k == k0 else x
    for k in range(n):
        w[k] = jnp.where(lane <= sub + 8 * k, w[k], 0.0)
    return upper, w


def corner_kernel(idx, cmap, corner, q, l_out, li_out, x_out, w, ut, xs):
    s, r, c = idx[0], idx[1], idx[2]
    core = c % 2
    y = c // 2
    for kk in range(2):
        for p in range(4):
            at = 64 * (2 * ((y + OFFS[p]) % 4) + (core if kk == 0 else 1 - core))
            w[pl.ds(pl.multiple_of(at, 64), 64), :] = corner[kk * 4 + p]
    xs[...] = jnp.zeros_like(xs)
    for i in range(4):
        child = (s + OFFS[i]) % 4
        for j in range(4):
            row = (r + OFFS[j]) % 4
            slot = cmap[child * 64 + row * 16]
            chunk = jnp.where(core == 0, i * 4 + j, j * 4 + i)

            @pl.when(slot < 4)
            def _():
                hi, lo = split(q[chunk])
                at = pl.ds(pl.multiple_of(slot * B, B), B)
                xs[i, at, 0:K] = hi
                xs[i, at, K : 2 * K] = lo
    for i in range(4):
        hi, lo = xs[i, :, 0:K], xs[i, :, K : 2 * K]
        x_out[i, :, 0:K] = hi
        x_out[i, :, K : 2 * K] = hi
        x_out[i, :, 2 * K :] = lo
        a = jnp.concatenate([hi, lo, hi], axis=1)
        b = jnp.concatenate([hi, hi, lo], axis=1)
        w[...] -= dot_t(a, b)

    col = lax.broadcasted_iota(jnp.int32, (B, PW), 1)
    row = lax.broadcasted_iota(jnp.int32, (B, B), 0)
    col_b = lax.broadcasted_iota(jnp.int32, (B, B), 1)
    eye = jnp.where(row == col_b, 1.0, 0.0).astype(F32)

    def stage(b, carry):
        o = pl.multiple_of(b * B, B)
        blk = pl.ds(o, B)
        diag = w[blk, blk]
        upper, inv = factor_block([diag[8 * k : 8 * k + 8, :] for k in range(16)])
        inv = jnp.concatenate(inv, axis=0)
        w[blk, blk] = eye
        u = jnp.dot(inv, w[blk, :], precision=lax.Precision.HIGHEST, preferred_element_type=F32)
        right = jnp.where(col >= o + B, u, 0.0)
        ut[blk, :] = right
        ut[blk, blk] = jnp.concatenate(upper, axis=0)
        w[:, blk] = jnp.zeros((PW, B), F32)
        w[...] -= lax.dot_general(
            right,
            u,
            (((0,), (0,)), ((), ())),
            precision=lax.Precision.HIGHEST,
            preferred_element_type=F32,
        )
        w[blk, :] = u
        return carry

    lax.fori_loop(0, 4, stage, 0)
    rows = lax.broadcasted_iota(jnp.int32, (PW, PW), 0)
    cols = lax.broadcasted_iota(jnp.int32, (PW, PW), 1)
    li_out[...] = right_cat(jnp.where(cols <= rows, w[...], 0.0))
    l_out[...] = ut[...].T


def tile_kernel(
    idx, cmap, s0, s1, s2, s3, rows_ref, pg_ref, x_ref, l_ref, li_ref, parent, out, own_out,
    acc, pg, pc, rcat, ocat, fcat, sem,
):
    s, r, c = idx[0], idx[1], idx[2]
    core = c % 2
    group = s * 4 + r
    i = pl.program_id(0)
    tile_rows, tile_cols = parent.shape
    load = pltpu.make_async_copy(parent, acc.at[pl.ds(0, tile_rows), :], sem.at[0])

    @pl.when(i == 0)
    def _():
        load.start()
        pc[...] = jnp.zeros_like(pc)
        for o in range(8):
            pg[pl.ds(64 * o, 64), :] = pg_ref[o, 0:64, :]
            pg[pl.ds(512 + 64 * o, 64), :] = pg_ref[o, 64:128, :]

    child = (s + offset(i)) % 4
    rcat[...] = left_cat(rows_ref[...].reshape(tile_rows, K))
    x = x_ref[0]

    def row_slot(rr, e):
        v = cmap[child * 64 + rr * 16 + (group // 2) * 2 + e] - group * 8
        return jnp.where((v >= 0) & (v < 8), v, 8)

    def to_rows(dst, value, cols):
        for rr in range(4):
            for e in range(2):
                at = row_slot(rr, e) * B
                for part in range(4):
                    src = (4 * e + part) * B + rr * 32
                    d = pl.ds(pl.multiple_of(at + 32 * part, 32), 32)
                    dst[d, cols] -= value[src : src + 32, :]

    for h in range(2):
        cols = slice(256 * h, 256 * h + 256)
        to_rows(pg, dot_t(rcat[...], x_ref[0, cols, :]), cols)

    @pl.when(i == 0)
    def _():
        load.wait()

    for j, piece in enumerate((s0, s1, s2, s3)):
        rr = (r + OFFS[j]) % 4
        p_sub = jnp.where(core == 0, child, child)
        shard = (p_sub * 4 + rr)
        at = (shard // 8) * 1024 + 64 * (shard % 8)
        pc[pl.ds(pl.multiple_of(at, 64), 64), :] += piece[0, 256:320, :]
        pc[pl.ds(pl.multiple_of(at + 512, 64), 64), :] += piece[0, 320:384, :]
        hi, lo = split(piece[0, 0:256, :])
        scat = jnp.concatenate([hi, hi, lo], axis=1)
        prod = dot_t(rcat[...], scat)
        up = dot_t(jnp.concatenate([hi, lo, hi], axis=1), x)
        for e in range(2):
            slot = cmap[child * 64 + rr * 16 + c * 2 + e] - c * 16
            at = pl.multiple_of(slot * B, B)
            pc[pl.ds(at, B), :] -= up[B * e : B * e + B, :]
            to_rows(acc, prod[:, B * e : B * e + B], pl.ds(at, B))

    @pl.when(i == 3)
    def _():
        li = li_ref[...]
        own = dot_t(left_cat(pg[pl.ds(0, tile_rows), :]), li)
        pg[pl.ds(0, tile_rows), :] = own

        @pl.when(group == 0)
        def _():
            pg[pl.ds(0, PW), :] = l_ref[...]

        ocat[...] = left_cat(pg[pl.ds(0, tile_rows), :])
        send_own = pltpu.make_async_copy(pg.at[pl.ds(0, tile_rows), :], own_out, sem.at[1])
        send_own.start()
        for n in range(tile_cols // 256):
            cols = pl.ds(256 * n, 256)
            far = dot_t(left_cat(pc[cols, :]), li)
            if n < 2:
                far = jnp.where(c == 0, l_ref[cols, :], far)
            fcat[...] = right_cat(far)
            acc[pl.ds(0, tile_rows), cols] -= dot_t(ocat[...], fcat[...])
            pltpu.make_async_copy(
                acc.at[pl.ds(0, tile_rows), cols], out.at[:, cols], sem.at[2]
            ).start()
        pltpu.make_async_copy(acc.at[pl.ds(0, tile_rows), :], out, sem.at[2]).wait()
        send_own.wait()


def per_device(parent_front, child_panel, child_pattern, child_map):
    s = lax.axis_index("sub")
    r = lax.axis_index("row")
    c = lax.axis_index("col")
    y, core = c // 2, c % 2
    idx = jnp.stack([s, r, c]).astype(jnp.int32)
    cmap = child_map.reshape(-1)
    tile_rows, tile_cols = parent_front.shape
    panel = child_panel[0]
    weights = jnp.repeat(child_pattern[0].astype(F32), B, axis=1)

    q = ring_gather(panel[:B] * weights[0][None, :])

    slabs = parent_front[:, :PW].reshape(2, 8, 64, PW).transpose(1, 0, 2, 3).reshape(4, 2, B, PW)
    mate = permute(slabs[:, 1], move_pairs("k", 1, lambda s, r, c: c == 0))
    mine = jnp.where(core == 0, slabs[:, 0], mate)
    near_y = lambda s, r, c: c < 2
    share = jnp.where(y == 0, mine[0], jnp.zeros_like(mine[0]))
    for k in (1, 3, 2):
        share = share + permute(mine[k], move_pairs("y", k, near_y))

    slab = share[:64]
    at_root = (lambda s, r, c: s == 0 and r == 0)
    on_line = (lambda s, r, c: (s == 0) if c % 2 else (r == 0))

    def first_axis_is_root(s, r, c):
        return s == 0 and r == 0

    def second_axis_is_root(s, r, c):
        return r == 0 if axis_of(1, c) == "z" else s == 0

    here = jnp.where((s == 0) & (r == 0), slab, jnp.zeros_like(slab))
    one = here
    for k in (1, 3, 2):
        one = one + permute(here, pairs(0, k, first_axis_is_root))
    two = one
    for k in (1, 3, 2):
        two = two + permute(one, pairs(1, k, second_axis_is_root))
    ring_y = [two] + [permute(two, move_pairs("y", k)) for k in (1, 3, 2)]
    ring_y = jnp.stack([ring_y[0], ring_y[1], ring_y[2], ring_y[3]])
    corner = jnp.concatenate([ring_y, permute(ring_y, move_pairs("k", 1))], axis=0)

    oct_rows = lax.dynamic_slice_in_dim(panel.reshape(8, 8, 32, K), c, 1, 1)[:, 0]
    oct_w = weights.reshape(8, 2, K)
    oct_w = jnp.where(c >= 4, oct_w[:, 1], oct_w[:, 0])
    outgoing = jnp.repeat(oct_rows * oct_w[:, None, :], 2, axis=0)
    arrived = lax.all_to_all(outgoing, ("sub", "row"), split_axis=0, concat_axis=0, tiled=True)
    row_share = jnp.concatenate([arrived.reshape(16 * 32, K), share], axis=0)
    row_data = lax.all_gather(row_share, "col", axis=0, tiled=False)

    to_shard = []
    for g in range(16):
        for cc in range(8):
            b = 8 * g + cc
            to_shard.append((g * 8 + cc, (b % 16) * 8 + b // 16))
    panel_share = permute(share, to_shard)
    own_rows = lax.dynamic_slice_in_dim(panel, c * (E * B), E * B, 0).reshape(E, B, K)
    own_w = lax.dynamic_slice_in_dim(weights, c * E, E, 0)
    col_share = jnp.concatenate([(own_rows * own_w[:, None, :]).reshape(E * B, K), panel_share], axis=0)
    col_data = ring_gather(col_share).reshape(16, 3 * B, K)

    vmem = pl.BlockSpec(memory_space=pltpu.VMEM)
    smem = pl.BlockSpec(memory_space=pltpu.SMEM)
    lower, lower_inv, x_cat = pl.pallas_call(
        corner_kernel,
        in_specs=[smem, smem, vmem, vmem],
        out_specs=[vmem, vmem, vmem],
        out_shape=[
            jax.ShapeDtypeStruct((PW, PW), F32),
            jax.ShapeDtypeStruct((PW, 3 * PW), BF16),
            jax.ShapeDtypeStruct((4, PW, 3 * K), BF16),
        ],
        scratch_shapes=[
            pltpu.VMEM((PW, PW), F32),
            pltpu.VMEM((PW, PW), F32),
            pltpu.VMEM((4, PW, 2 * K), BF16),
        ],
        compiler_params=pltpu.CompilerParams(vmem_limit_bytes=40 * MIB),
        cost_estimate=pl.CostEstimate(flops=60_000_000_000, bytes_accessed=12 * MIB, transcendentals=0),
    )(idx, cmap, corner, q.reshape(16, B, K))

    def chunk_map(j):
        def at(i, idx, cmap):
            first = i * 4 + j
            second = j * 4 + i
            return (jnp.where(idx[2] % 2 == 0, first, second), 0, 0)
        return at

    def child_rows(i, idx, cmap):
        return (0, (idx[0] + offset(i)) % 4, 0)

    hbm = pl.BlockSpec(memory_space=pl.ANY)
    once = pl.Buffered(1)
    schur, own = pl.pallas_call(
        tile_kernel,
        grid_spec=pltpu.PrefetchScalarGridSpec(
            num_scalar_prefetch=2,
            grid=(4,),
            in_specs=[pl.BlockSpec((1, 3 * B, K), chunk_map(j)) for j in range(4)]
            + [
                pl.BlockSpec((8, B, K), child_rows),
                pl.BlockSpec((8, B, K), lambda i, idx, cmap: (0, 4, 0), pipeline_mode=once),
                pl.BlockSpec((1, PW, 3 * K), lambda i, idx, cmap: (i, 0, 0)),
                pl.BlockSpec((PW, PW), lambda i, idx, cmap: (0, 0), pipeline_mode=once),
                pl.BlockSpec((PW, 3 * PW), lambda i, idx, cmap: (0, 0), pipeline_mode=once),
                hbm,
            ],
            out_specs=[hbm, hbm],
            scratch_shapes=[
                pltpu.VMEM((tile_rows + B, tile_cols), F32),
                pltpu.VMEM((tile_rows + B, PW), F32),
                pltpu.VMEM((tile_cols, PW), F32),
                pltpu.VMEM((tile_rows, 3 * K), BF16),
                pltpu.VMEM((tile_rows, 3 * K), BF16),
                pltpu.VMEM((256, 3 * K), BF16),
                pltpu.SemaphoreType.DMA((3,)),
            ],
        ),
        out_shape=[
            jax.ShapeDtypeStruct((tile_rows, tile_cols), F32),
            jax.ShapeDtypeStruct((tile_rows, PW), F32),
        ],
        compiler_params=pltpu.CompilerParams(
            vmem_limit_bytes=56 * MIB, dimension_semantics=("arbitrary",)
        ),
        cost_estimate=pl.CostEstimate(flops=45_000_000_000, bytes_accessed=50 * MIB, transcendentals=0),
    )(idx, cmap, col_data, col_data, col_data, col_data, row_data, row_data, x_cat, lower, lower_inv, parent_front)
    return schur, own


def solution(mesh):
    placed = (P(("sub", "row"), "col"), P("sub", "row", None), P("sub", "row", None), P())
    return jax.shard_map(
        per_device,
        mesh=mesh,
        in_specs=placed,
        out_specs=(P(("sub", "row"), "col"), P(("sub", "row"), None)),
        check_vma=False,
    )
```

time: 931 us -> 307 us (0.33)
  waiting for transfers between devices: 574 us -> 57 us
  other arithmetic: 206 us -> 9.03 us
  Pallas kernels: 0 us -> 108 us
  starting transfers between devices: 6.38 us -> 81.2 us
  matrix products: 47 us -> 0 us
  local copies, waits for them, and re-layouts: 70.9 us -> 34.3 us
    all_to_all x1, waiting for transfers between devices: 281 us -> 0.01 us  [per_device(): lax.all_to_all(outgoing, ('sub', 'row'), split_axis=0, concat_axis=0, til...]
    psum x3 -> x0, waiting for transfers between devices: 260 us -> none  [broadcast(): return lax.psum(jnp.where(mine, x, jnp.zeros_like(x)), axis)]
    another operation x18 -> x2, other arithmetic: 120 us -> 0.11 us  [the longest x1 0.08 us: per_device(): idx = jnp.stack([s, r, c]).astype(jnp.int32)]
    pallas_call x0 -> x2, Pallas kernels: none -> 108 us  [the longest x1 64.5 us: per_device(): pl.pallas_call(tile_kernel, grid_spec=pltpu.PrefetchScalarGridSpec(num_sc...]
    ppermute x0 -> x31, starting transfers between devices: none -> 72.7 us  [permute(): return lax.ppermute(x, ALL, prs)]
    ppermute x0 -> x31, waiting for transfers between devices: none -> 57 us  [permute(): return lax.ppermute(x, ALL, prs)]
    scatter-add x1 -> x0, other arithmetic: 50.6 us -> none  [per_device(): summed.at[row_slot[:, :, None], :, col_slot[:, None, :], :]]
    dot_general x2 -> x0, matrix products: 36.9 us -> none  [the longest x1 19 us: per_device(): lax.dot_general(own_factor, far_rows, (((1,), (1,)), ((), ())), precision...]
  transfers between devices with their start and end apart: 5 -> 33, of which waited for: 5 -> 13; matrix products, arithmetic and copies ran while one was open for 2% -> 13% of each run, Pallas kernels for 0% -> 14%
where the time goes in v1:
time: 307 us; the launch traced here: 304 us
  Pallas kernels  108 us (35%)
  starting transfers between devices  81.2 us (26%)
  waiting for transfers between devices  57 us (19%)
  local copies, waits for them, and re-layouts  34.3 us (11%)
  between operations  14.7 us (5%)
  other arithmetic  9.03 us (3%)
    ppermute x31, starting transfers between devices, permute(): return lax.ppermute(x, ALL, prs)  72.7 us
    pallas_call x1, Pallas kernels, per_device(): pl.pallas_call(tile_kernel, grid_spec=pltpu.PrefetchScalarGridSpec(num_sc...  64.5 us
    ppermute x31, waiting for transfers between devices, permute(): return lax.ppermute(x, ALL, prs)  57 us
    pallas_call x1, Pallas kernels, per_device(): pl.pallas_call(corner_kernel, in_specs=[smem, smem, vmem, vmem], out_spec...  43.5 us
    unnamed x37, local copies, waits for them, and re-layouts  23 us
    all_to_all x1, starting transfers between devices, per_device(): lax.all_to_all(outgoing, ('sub', 'row'), split_axis=0, concat_axis=0, til...  8.46 us
  transfers between devices with their start and end apart: 33, of which 13 were waited for; matrix products, arithmetic and copies ran while one was open for 13% of the time, Pallas kernels for 14%

profile of v1, /device:TPU:0, one launch (start us, length us, event | category | flops | bytes accessed | tf_op | source)
XLA Modules:
  0.0 304.2 jit_solution(2171278619528246009)
XLA Ops:
  7.2 1.6 slice-done
  9.0 2.3 collective-permute-start
  13.8 8.5 %all-to-all-start = ((f32[16,32,512]{2,1,0:T(8,128)}), f32[16,32,512]{2,1,0:T(8,128)}, u32[]{:S(2)}, u32[]{:S(2)}) async-start(f32[16,32,512]{2,1,0:T(8,128)} %bitcast.18), calls=%async_computation | async-start | bytes 2097152 | tf_op jit(solution)/shard_map/all_to_all | solution.py:366
  22.7 4.0 %collective-permute-start.3 = (f32[128,512]{1,0:T(8,128)S(1)}, f32[128,512]{1,0:T(8,128)S(1)}, u32[]{:S(2)}, u32[]{:S(2)}) collective-permute-start(f32[128,512]{1,0:T(8,128)S(1)} %get-tuple-element.13), channel_id=1, source_target_pairs={{0,4},{1,5},{8,12},{9,13},{16,20},{17,21},{24,28},{25,29},{32,36},... | collective-permute-start | bytes 786440 | tf_op jit(solution)/shard_map/ppermute | solution.py:54
  26.7 1.3 collective-permute-start.2
  28.0 1.3 collective-permute-start.1
  29.4 4.0 %collective-permute-done.3 = f32[128,512]{1,0:T(8,128)S(1)} collective-permute-done((f32[128,512]{1,0:T(8,128)S(1)}, f32[128,512]{1,0:T(8,128)S(1)}, u32[]{:S(2)}, u32[]{:S(2)}) %collective-permute-start.3) | collective-permute-done | bytes 262176 | tf_op jit(solution)/shard_map/ppermute | solution.py:54
  34.5 4.3 %collective-permute-done.1 = f32[128,512]{1,0:T(8,128)S(1)} collective-permute-done((f32[128,512]{1,0:T(8,128)S(1)}, f32[128,512]{1,0:T(8,128)S(1)}, u32[]{:S(2)}, u32[]{:S(2)}) %collective-permute-start.1) | collective-permute-done | bytes 262176 | tf_op jit(solution)/shard_map/ppermute | solution.py:54
  38.9 2.4 pad_maximum_fusion
  42.0 2.2 constant_dynamic-update-slice_fusion.5
  44.3 9.7 %collective-permute-start.5 = (f32[384,512]{1,0:T(8,128)S(1)}, f32[384,512]{1,0:T(8,128)S(1)}, u32[]{:S(2)}, u32[]{:S(2)}) collective-permute-start(f32[384,512]{1,0:T(8,128)S(1)} %pad_maximum_fusion.1), channel_id=1, source_target_pairs={{0,8},{1,33},{2,10},{3,35},{4,12},{5,37},{6,14},{7,39},{8,16},{9,4... | collective-permute-start | bytes 2359304 | tf_op jit(solution)/shard_map/ppermute | solution.py:54
  54.2 2.1 collective-permute-start.6
  56.3 1.7 constant_dynamic-update-slice_fusion.25
  58.0 1.5 collective-permute-start.23
  59.5 1.8 collective-permute-start.24
  62.0 6.9 %collective-permute-done.23 = f32[128,512]{1,0:T(8,128)S(1)} collective-permute-done((f32[128,512]{1,0:T(8,128)S(1)}, f32[128,512]{1,0:T(8,128)S(1)}, u32[]{:S(2)}, u32[]{:S(2)}) %collective-permute-start.23) | collective-permute-done | bytes 262176 | tf_op jit(solution)/shard_map/ppermute | solution.py:54
  70.5 1.9 collective-permute-start.26
  73.6 3.1 %collective-permute-start.8 = (f32[192,512]{1,0:T(8,128)S(1)}, f32[192,512]{1,0:T(8,128)S(1)}, u32[]{:S(2)}, u32[]{:S(2)}) collective-permute-start(f32[192,512]{1,0:T(8,128)S(1)} %slice.97), channel_id=1, source_target_pairs={{0,24},{1,97},{2,26},{3,99},{4,28},{5,101},{6,30},{7,103},{8,0},{9... | collective-permute-start | bytes 1179656 | tf_op jit(solution)/shard_map/ppermute | solution.py:54
  76.7 1.4 constant_dynamic-update-slice_fusion.3
  78.1 1.4 constant_dynamic-update-slice_fusion.2
  79.5 1.9 collective-permute-done.7
  83.4 9.7 %collective-permute-start.9 = (f32[1536,512]{1,0:T(8,128)}, f32[1536,512]{1,0:T(8,128)S(1)}, u32[]{:S(2)}, u32[]{:S(2)}) collective-permute-start(f32[1536,512]{1,0:T(8,128)} %get-tuple-element.21), channel_id=1, source_target_pairs={{0,32},{1,9},{2,34},{3,11},{4,36},{5,13},{6,38},{7,15},{8,40},{9,1... | collective-permute-start | bytes 9437192 | tf_op jit(solution)/shard_map/ppermute | solution.py:54
  93.1 5.4 %collective-permute-start.10 = (f32[1536,512]{1,0:T(8,128)}, f32[1536,512]{1,0:T(8,128)}, u32[]{:S(2)}, u32[]{:S(2)}) collective-permute-start(f32[1536,512]{1,0:T(8,128)} %get-tuple-element.21), channel_id=1, source_target_pairs={{0,96},{1,25},{2,98},{3,27},{4,100},{5,29},{6,102},{7,31},{8,104},... | collective-permute-start | bytes 9437192 | tf_op jit(solution)/shard_map/ppermute | solution.py:54
  101.6 3.2 %collective-permute-start.28 = (f32[512,512]{1,0:T(8,128)}, f32[512,512]{1,0:T(8,128)}, u32[]{:S(2)}, u32[]{:S(2)}) collective-permute-start(f32[512,512]{1,0:T(8,128)} %get-tuple-element.31), channel_id=1, source_target_pairs={{0,96},{1,25},{2,98},{3,27},{4,100},{5,29},{6,102},{7,31},{8,104},... | collective-permute-start | bytes 3145736 | tf_op jit(solution)/shard_map/ppermute | solution.py:54
  104.9 3.4 %collective-permute-start.15 = (f32[64,512]{1,0:T(8,128)S(1)}, f32[64,512]{1,0:T(8,128)S(1)}, u32[]{:S(2)}, u32[]{:S(2)}) collective-permute-start(f32[64,512]{1,0:T(8,128)S(1)} %slice_select_fusion.1), channel_id=1, source_target_pairs={{0,16},{1,65},{2,18},{3,67},{4,20},{5,69},{6,22},{7,71}} | collective-permute-start | bytes 393224 | tf_op jit(solution)/shard_map/ppermute | solution.py:54
  108.3 3.9 %collective-permute-done.15 = f32[64,512]{1,0:T(8,128)S(1)} collective-permute-done((f32[64,512]{1,0:T(8,128)S(1)}, f32[64,512]{1,0:T(8,128)S(1)}, u32[]{:S(2)}, u32[]{:S(2)}) %collective-permute-start.15) | collective-permute-done | bytes 131104 | tf_op jit(solution)/shard_map/ppermute | solution.py:54
  112.2 1.3 collective-permute-start.14
  113.5 3.9 %collective-permute-done.14 = f32[64,512]{1,0:T(8,128)S(1)} collective-permute-done((f32[64,512]{1,0:T(8,128)S(1)}, f32[64,512]{1,0:T(8,128)S(1)}, u32[]{:S(2)}, u32[]{:S(2)}) %collective-permute-start.14) | collective-permute-done | bytes 131104 | tf_op jit(solution)/shard_map/ppermute | solution.py:54
  118.1 1.9 collective-permute-start.13
  120.2 3.1 %collective-permute-done.13 = f32[64,512]{1,0:T(8,128)} collective-permute-done((f32[64,512]{1,0:T(8,128)S(1)}, f32[64,512]{1,0:T(8,128)}, u32[]{:S(2)}, u32[]{:S(2)}) %collective-permute-start.13) | collective-permute-done | bytes 131104 | tf_op jit(solution)/shard_map/ppermute | solution.py:54
  124.4 1.3 collective-permute-start.18
  125.7 19.6 %collective-permute-done.27 = f32[512,512]{1,0:T(8,128)} collective-permute-done((f32[512,512]{1,0:T(8,128)}, f32[512,512]{1,0:T(8,128)}, u32[]{:S(2)}, u32[]{:S(2)}) %collective-permute-start.27) | collective-permute-done | bytes 1048608 | tf_op jit(solution)/shard_map/ppermute | solution.py:54
  145.2 3.9 %collective-permute-start.17 = (f32[64,512]{1,0:T(8,128)S(1)}, f32[64,512]{1,0:T(8,128)S(1)}, u32[]{:S(2)}, u32[]{:S(2)}) collective-permute-start(f32[64,512]{1,0:T(8,128)S(1)} %add_add_fusion.1), channel_id=1, source_target_pairs={{0,96},{1,25},{2,98},{3,27},{4,100},{5,29},{6,102},{7,31},{8,104},... | collective-permute-start | bytes 393224 | tf_op jit(solution)/shard_map/ppermute | solution.py:54
  150.3 1.3 collective-permute-start.16
  152.6 2.3 constant_dynamic-update-slice_fusion.29
  155.1 3.2 %collective-permute-start.20 = (f32[64,512]{1,0:T(8,128)S(1)}, f32[64,512]{1,0:T(8,128)S(1)}, u32[]{:S(2)}, u32[]{:S(2)}) collective-permute-start(f32[64,512]{1,0:T(8,128)S(1)} %get-tuple-element.11), channel_id=1, source_target_pairs={{0,6},{1,7},{2,0},{3,1},{4,2},{5,3},{6,4},{7,5},{8,14},{9,15},{10,... | collective-permute-start | bytes 393224 | tf_op jit(solution)/shard_map/ppermute | solution.py:54
  158.3 2.3 constant_dynamic-update-slice_fusion.28
  161.2 1.6 collective-permute-start.29
  162.8 1.7 collective-permute-start.30
  164.9 6.7 %collective-permute-done.29 = f32[256,512]{1,0:T(8,128)S(1)} collective-permute-done((f32[256,512]{1,0:T(8,128)S(1)}, f32[256,512]{1,0:T(8,128)S(1)}, u32[]{:S(2)}, u32[]{:S(2)}) %collective-permute-start.29) | collective-permute-done | bytes 524320 | tf_op jit(solution)/shard_map/ppermute | solution.py:54
  174.0 1.5 slice.99
  175.6 3.0 %collective-permute-start.12 = (f32[768,512]{1,0:T(8,128)S(1)}, f32[768,512]{1,0:T(8,128)S(1)}, u32[]{:S(2)}, u32[]{:S(2)}) collective-permute-start(f32[768,512]{1,0:T(8,128)S(1)} %slice.99), channel_id=1, source_target_pairs={{0,96},{1,25},{2,98},{3,27},{4,100},{5,29},{6,102},{7,31},{8,104},... | collective-permute-start | bytes 4718600 | tf_op jit(solution)/shard_map/ppermute | solution.py:54
  178.6 43.5 %shard_map.59 = (f32[512,512]{1,0:T(8,128)S(1)}, bf16[512,1536]{1,0:T(8,128)(2,1)S(1)}, bf16[4,512,1536]{2,1,0:T(8,128)(2,1)S(1)}) custom-call(s32[3]{0:T(128)S(1)} %pad_add_fusion.idx, s32[256]{0:T(256)S(1)} %reshape.48.cmap, f32[8,64,512]{2,1,0:T(8,128)S(1)} %constant_dynamic-update-slice_fusion.16.corner, f32[16,128,512]{2,1,0:T(8,128)} %bitcast.27.q), custom_call_target="tpu_custom_call" | custom-call | flops 60000002048 | bytes 12582912 | tf_op jit(solution)/shard_map/pallas_call | solution.py:383
  222.1 2.3 constant_dynamic-update-slice_fusion.9
  224.4 5.6 %constant_dynamic-update-slice_fusion.8 = f32[6144,512]{1,0:T(8,128)} fusion(f32[6144,512]{1,0:T(8,128)} %constant_dynamic-update-slice_fusion.9, f32[1536,512]{1,0:T(8,128)} %collective-permute-done.10), kind=kLoop, calls=%fused_computation.28 | loop fusion | bytes 6291456
  230.0 1.3 constant_dynamic-update-slice_fusion.7
  231.3 1.3 constant_dynamic-update-slice_fusion.6
  232.6 64.5 %shard_map.60 = (f32[1024,2048]{1,0:T(8,128)}, f32[1024,512]{1,0:T(8,128)}) custom-call(s32[3]{0:T(128)} %copy-done.1, s32[256]{0:T(256)} %copy-done, f32[16,384,512]{2,1,0:T(8,128)} %bitcast.76, f32[16,384,512]{2,1,0:T(8,128)} %bitcast.77, f32[16,384,512]{2,1,0:T(8,128)} %bitcast.78, f32[16,384,512]{2,1,0:T(8,128)} %bitcast.79, f32[8,640,512]{2,1,0:T(8,128)} %bitcast.80, ...), custom_call_target="tpu_custom_call" | custom-call | flops 44999999488 | bytes 52428800 | tf_op jit(solution)/shard_map/pallas_call | solution.py:413
  (98 shorter events, 21.7 us)
Async XLA Ops:
  7.2 1.6 slice-start
  7.2 4.2 %copy-start.7 = (s32[1,16,4]{1,2,0:T(4,128)S(1)}, s32[1,16,4]{1,2,0:T(4,128)}, u32[]{:S(2)}) copy-start(s32[1,16,4]{1,2,0:T(4,128)} %param.6) | copy-start | bytes 772
  9.0 13.3 %collective-permute-start = (f32[4,128,512]{2,1,0:T(8,128)S(1)}, f32[4,128,512]{2,1,0:T(8,128)}, u32[]{:S(2)}, u32[]{:S(2)}) collective-permute-start(f32[4,128,512]{2,1,0:T(8,128)S(1)} %slice_bitcast_fusion), channel_id=1, source_target_pairs={{0,1},{8,9},{16,17},{24,25},{32,33},{40,41},{48,49},{56,57},{64,65... | collective-permute-start | bytes 3145736 | tf_op jit(solution)/shard_map/ppermute | solution.py:54
  13.8 25.1 %all-to-all-start = ((f32[16,32,512]{2,1,0:T(8,128)}), f32[16,32,512]{2,1,0:T(8,128)}, u32[]{:S(2)}, u32[]{:S(2)}) async-start(f32[16,32,512]{2,1,0:T(8,128)} %bitcast.18), calls=%async_computation | async-start | bytes 2097152 | tf_op jit(solution)/shard_map/all_to_all | solution.py:366
  22.3 210.3 %all-gather.3.cloned.1.call-start = ((), (), s32[]{:S(2)}) async-start(), calls=%async_computation.1 | async-start | bytes 11796480 | tf_op jit(solution)/shard_map/all_gather | solution.py:368
  22.7 10.7 %collective-permute-start.3 = (f32[128,512]{1,0:T(8,128)S(1)}, f32[128,512]{1,0:T(8,128)S(1)}, u32[]{:S(2)}, u32[]{:S(2)}) collective-permute-start(f32[128,512]{1,0:T(8,128)S(1)} %get-tuple-element.13), channel_id=1, source_target_pairs={{0,4},{1,5},{8,12},{9,13},{16,20},{17,21},{24,28},{25,29},{32,36},... | collective-permute-start | bytes 786440 | tf_op jit(solution)/shard_map/ppermute | solution.py:54
  26.7 7.8 %collective-permute-start.2 = (f32[128,512]{1,0:T(8,128)S(1)}, f32[128,512]{1,0:T(8,128)S(1)}, u32[]{:S(2)}, u32[]{:S(2)}) collective-permute-start(f32[128,512]{1,0:T(8,128)S(1)} %get-tuple-element.14), channel_id=1, source_target_pairs={{0,6},{1,7},{8,14},{9,15},{16,22},{17,23},{24,30},{25,31},{32,38},... | collective-permute-start | bytes 786440 | tf_op jit(solution)/shard_map/ppermute | solution.py:54
  28.0 10.8 %collective-permute-start.1 = (f32[128,512]{1,0:T(8,128)S(1)}, f32[128,512]{1,0:T(8,128)S(1)}, u32[]{:S(2)}, u32[]{:S(2)}) collective-permute-start(f32[128,512]{1,0:T(8,128)S(1)} %get-tuple-element.12), channel_id=1, source_target_pairs={{0,2},{1,3},{8,10},{9,11},{16,18},{17,19},{24,26},{25,27},{32,34},... | collective-permute-start | bytes 786440 | tf_op jit(solution)/shard_map/ppermute | solution.py:54
  41.3 3.0 collective-permute-start.4
  44.3 28.1 %collective-permute-start.5 = (f32[384,512]{1,0:T(8,128)S(1)}, f32[384,512]{1,0:T(8,128)S(1)}, u32[]{:S(2)}, u32[]{:S(2)}) collective-permute-start(f32[384,512]{1,0:T(8,128)S(1)} %pad_maximum_fusion.1), channel_id=1, source_target_pairs={{0,8},{1,33},{2,10},{3,35},{4,12},{5,37},{6,14},{7,39},{8,16},{9,4... | collective-permute-start | bytes 2359304 | tf_op jit(solution)/shard_map/ppermute | solution.py:54
  54.2 19.4 %collective-permute-start.6 = (f32[384,512]{1,0:T(8,128)S(1)}, f32[384,512]{1,0:T(8,128)S(1)}, u32[]{:S(2)}, u32[]{:S(2)}) collective-permute-start(f32[384,512]{1,0:T(8,128)S(1)} %pad_maximum_fusion.1), channel_id=1, source_target_pairs={{0,24},{1,97},{2,26},{3,99},{4,28},{5,101},{6,30},{7,103},{8,0},{9... | collective-permute-start | bytes 2359304 | tf_op jit(solution)/shard_map/ppermute | solution.py:54
  58.0 10.8 %collective-permute-start.23 = (f32[128,512]{1,0:T(8,128)S(1)}, f32[128,512]{1,0:T(8,128)S(1)}, u32[]{:S(2)}, u32[]{:S(2)}) collective-permute-start(f32[128,512]{1,0:T(8,128)S(1)} %get-tuple-element.9), channel_id=1, source_target_pairs={{0,8},{1,33},{2,10},{3,35},{4,12},{5,37},{6,14},{7,39},{8,16},{9,4... | collective-permute-start | bytes 786440 | tf_op jit(solution)/shard_map/ppermute | solution.py:54
  59.5 11.0 %collective-permute-start.24 = (f32[128,512]{1,0:T(8,128)S(1)}, f32[128,512]{1,0:T(8,128)S(1)}, u32[]{:S(2)}, u32[]{:S(2)}) collective-permute-start(f32[128,512]{1,0:T(8,128)S(1)} %get-tuple-element.9), channel_id=1, source_target_pairs={{0,24},{1,97},{2,26},{3,99},{4,28},{5,101},{6,30},{7,103},{8,0},{9... | collective-permute-start | bytes 786440 | tf_op jit(solution)/shard_map/ppermute | solution.py:54
  68.9 31.3 %collective-permute-start.25 = (f32[64,512]{1,0:T(8,128)S(1)}, f32[64,512]{1,0:T(8,128)S(1)}, u32[]{:S(2)}, u32[]{:S(2)}) collective-permute-start(f32[64,512]{1,0:T(8,128)S(1)} %slice.103), channel_id=1, source_target_pairs={{0,8},{1,33},{2,10},{3,35},{4,12},{5,37},{6,14},{7,39},{8,16},{9,4... | collective-permute-start | bytes 393224 | tf_op jit(solution)/shard_map/ppermute | solution.py:54
  70.5 30.4 %collective-permute-start.26 = (f32[64,512]{1,0:T(8,128)S(1)}, f32[64,512]{1,0:T(8,128)S(1)}, u32[]{:S(2)}, u32[]{:S(2)}) collective-permute-start(f32[64,512]{1,0:T(8,128)S(1)} %slice.104), channel_id=1, source_target_pairs={{0,24},{1,97},{2,26},{3,99},{4,28},{5,101},{6,30},{7,103},{8,0},{9... | collective-permute-start | bytes 393224 | tf_op jit(solution)/shard_map/ppermute | solution.py:54
  72.4 9.1 %collective-permute-start.7 = (f32[192,512]{1,0:T(8,128)S(1)}, f32[192,512]{1,0:T(8,128)S(1)}, u32[]{:S(2)}, u32[]{:S(2)}) collective-permute-start(f32[192,512]{1,0:T(8,128)S(1)} %slice.96), channel_id=1, source_target_pairs={{0,8},{1,33},{2,10},{3,35},{4,12},{5,37},{6,14},{7,39},{8,16},{9,4... | collective-permute-start | bytes 1179656 | tf_op jit(solution)/shard_map/ppermute | solution.py:54
  73.6 8.8 %collective-permute-start.8 = (f32[192,512]{1,0:T(8,128)S(1)}, f32[192,512]{1,0:T(8,128)S(1)}, u32[]{:S(2)}, u32[]{:S(2)}) collective-permute-start(f32[192,512]{1,0:T(8,128)S(1)} %slice.97), channel_id=1, source_target_pairs={{0,24},{1,97},{2,26},{3,99},{4,28},{5,101},{6,30},{7,103},{8,0},{9... | collective-permute-start | bytes 1179656 | tf_op jit(solution)/shard_map/ppermute | solution.py:54
  78.1 41.9 %copy-start.8 = (s32[4,64]{1,0:T(4,128)S(1)}, s32[4,64]{1,0:T(4,128)}, u32[]{:S(2)}) copy-start(s32[4,64]{1,0:T(4,128)} %param.7) | copy-start | bytes 3076
  83.4 89.9 %collective-permute-start.9 = (f32[1536,512]{1,0:T(8,128)}, f32[1536,512]{1,0:T(8,128)S(1)}, u32[]{:S(2)}, u32[]{:S(2)}) collective-permute-start(f32[1536,512]{1,0:T(8,128)} %get-tuple-element.21), channel_id=1, source_target_pairs={{0,32},{1,9},{2,34},{3,11},{4,36},{5,13},{6,38},{7,15},{8,40},{9,1... | collective-permute-start | bytes 9437192 | tf_op jit(solution)/shard_map/ppermute | solution.py:54
  93.1 81.0 %collective-permute-start.10 = (f32[1536,512]{1,0:T(8,128)}, f32[1536,512]{1,0:T(8,128)}, u32[]{:S(2)}, u32[]{:S(2)}) collective-permute-start(f32[1536,512]{1,0:T(8,128)} %get-tuple-element.21), channel_id=1, source_target_pairs={{0,96},{1,25},{2,98},{3,27},{4,100},{5,29},{6,102},{7,31},{8,104},... | collective-permute-start | bytes 9437192 | tf_op jit(solution)/shard_map/ppermute | solution.py:54
  101.6 43.6 %collective-permute-start.27 = (f32[512,512]{1,0:T(8,128)}, f32[512,512]{1,0:T(8,128)}, u32[]{:S(2)}, u32[]{:S(2)}) collective-permute-start(f32[512,512]{1,0:T(8,128)} %get-tuple-element.31), channel_id=1, source_target_pairs={{0,32},{1,9},{2,34},{3,11},{4,36},{5,13},{6,38},{7,15},{8,40},{9,1... | collective-permute-start | bytes 3145736 | tf_op jit(solution)/shard_map/ppermute | solution.py:54
  101.6 48.6 %collective-permute-start.28 = (f32[512,512]{1,0:T(8,128)}, f32[512,512]{1,0:T(8,128)}, u32[]{:S(2)}, u32[]{:S(2)}) collective-permute-start(f32[512,512]{1,0:T(8,128)} %get-tuple-element.31), channel_id=1, source_target_pairs={{0,96},{1,25},{2,98},{3,27},{4,100},{5,29},{6,102},{7,31},{8,104},... | collective-permute-start | bytes 3145736 | tf_op jit(solution)/shard_map/ppermute | solution.py:54
  104.9 7.3 %collective-permute-start.15 = (f32[64,512]{1,0:T(8,128)S(1)}, f32[64,512]{1,0:T(8,128)S(1)}, u32[]{:S(2)}, u32[]{:S(2)}) collective-permute-start(f32[64,512]{1,0:T(8,128)S(1)} %slice_select_fusion.1), channel_id=1, source_target_pairs={{0,16},{1,65},{2,18},{3,67},{4,20},{5,69},{6,22},{7,71}} | collective-permute-start | bytes 393224 | tf_op jit(solution)/shard_map/ppermute | solution.py:54
  112.2 5.2 %copy-start.5 = (f32[64,512]{1,0:T(8,128)}, f32[64,512]{1,0:T(8,128)S(1)}, u32[]{:S(2)}) copy-start(f32[64,512]{1,0:T(8,128)S(1)} %collective-permute-done.15) | copy-start | bytes 393220
  112.2 5.2 %collective-permute-start.14 = (f32[64,512]{1,0:T(8,128)S(1)}, f32[64,512]{1,0:T(8,128)S(1)}, u32[]{:S(2)}, u32[]{:S(2)}) collective-permute-start(f32[64,512]{1,0:T(8,128)S(1)} %slice_select_fusion.1), channel_id=1, source_target_pairs={{0,24},{1,97},{2,26},{3,99},{4,28},{5,101},{6,30},{7,103}} | collective-permute-start | bytes 393224 | tf_op jit(solution)/shard_map/ppermute | solution.py:54
  117.4 0.7 copy-start.6
  118.1 5.2 %collective-permute-start.13 = (f32[64,512]{1,0:T(8,128)S(1)}, f32[64,512]{1,0:T(8,128)}, u32[]{:S(2)}, u32[]{:S(2)}) collective-permute-start(f32[64,512]{1,0:T(8,128)S(1)} %slice_select_fusion.1), channel_id=1, source_target_pairs={{0,8},{1,33},{2,10},{3,35},{4,12},{5,37},{6,14},{7,39}} | collective-permute-start | bytes 393224 | tf_op jit(solution)/shard_map/ppermute | solution.py:54
  120.1 58.5 %copy-start = (s32[256]{0:T(256)}, s32[256]{0:T(256)S(1)}, u32[]{:S(2)}) copy-start(s32[256]{0:T(256)S(1)} %reshape.48.cmap) | copy-start | bytes 3076
  120.2 58.5 %copy-start.1 = (s32[3]{0:T(128)}, s32[3]{0:T(128)S(1)}, u32[]{:S(2)}) copy-start(s32[3]{0:T(128)S(1)} %pad_add_fusion.idx) | copy-start | bytes 40
  124.4 30.6 %collective-permute-start.18 = (f32[64,512]{1,0:T(8,128)S(1)}, f32[64,512]{1,0:T(8,128)S(1)}, u32[]{:S(2)}, u32[]{:S(2)}) collective-permute-start(f32[64,512]{1,0:T(8,128)S(1)} %add_add_fusion.1), channel_id=1, source_target_pairs={{0,64},{1,17},{2,66},{3,19},{4,68},{5,21},{6,70},{7,23},{8,72},{10... | collective-permute-start | bytes 393224 | tf_op jit(solution)/shard_map/ppermute | solution.py:54
  145.2 9.7 %collective-permute-start.17 = (f32[64,512]{1,0:T(8,128)S(1)}, f32[64,512]{1,0:T(8,128)S(1)}, u32[]{:S(2)}, u32[]{:S(2)}) collective-permute-start(f32[64,512]{1,0:T(8,128)S(1)} %add_add_fusion.1), channel_id=1, source_target_pairs={{0,96},{1,25},{2,98},{3,27},{4,100},{5,29},{6,102},{7,31},{8,104},... | collective-permute-start | bytes 393224 | tf_op jit(solution)/shard_map/ppermute | solution.py:54
  150.3 4.7 %collective-permute-start.16 = (f32[64,512]{1,0:T(8,128)S(1)}, f32[64,512]{1,0:T(8,128)S(1)}, u32[]{:S(2)}, u32[]{:S(2)}) collective-permute-start(f32[64,512]{1,0:T(8,128)S(1)} %add_add_fusion.1), channel_id=1, source_target_pairs={{0,32},{1,9},{2,34},{3,11},{4,36},{5,13},{6,38},{7,15},{8,40},{10,... | collective-permute-start | bytes 393224 | tf_op jit(solution)/shard_map/ppermute | solution.py:54
  155.0 6.2 %collective-permute-start.19 = (f32[64,512]{1,0:T(8,128)S(1)}, f32[64,512]{1,0:T(8,128)S(1)}, u32[]{:S(2)}, u32[]{:S(2)}) collective-permute-start(f32[64,512]{1,0:T(8,128)S(1)} %get-tuple-element.11), channel_id=1, source_target_pairs={{0,2},{1,3},{2,4},{3,5},{4,6},{5,7},{6,0},{7,1},{8,10},{9,11},{10,... | collective-permute-start | bytes 393224 | tf_op jit(solution)/shard_map/ppermute | solution.py:54
  155.1 7.7 %collective-permute-start.20 = (f32[64,512]{1,0:T(8,128)S(1)}, f32[64,512]{1,0:T(8,128)S(1)}, u32[]{:S(2)}, u32[]{:S(2)}) collective-permute-start(f32[64,512]{1,0:T(8,128)S(1)} %get-tuple-element.11), channel_id=1, source_target_pairs={{0,6},{1,7},{2,0},{3,1},{4,2},{5,3},{6,4},{7,5},{8,14},{9,15},{10,... | collective-permute-start | bytes 393224 | tf_op jit(solution)/shard_map/ppermute | solution.py:54
  158.3 6.5 %collective-permute-start.21 = (f32[64,512]{1,0:T(8,128)S(1)}, f32[64,512]{1,0:T(8,128)S(1)}, u32[]{:S(2)}, u32[]{:S(2)}) collective-permute-start(f32[64,512]{1,0:T(8,128)S(1)} %get-tuple-element.11), channel_id=1, source_target_pairs={{0,4},{1,5},{2,6},{3,7},{4,0},{5,1},{6,2},{7,3},{8,12},{9,13},{10,... | collective-permute-start | bytes 393224 | tf_op jit(solution)/shard_map/ppermute | solution.py:54
  161.2 10.4 %collective-permute-start.29 = (f32[256,512]{1,0:T(8,128)S(1)}, f32[256,512]{1,0:T(8,128)S(1)}, u32[]{:S(2)}, u32[]{:S(2)}) collective-permute-start(f32[256,512]{1,0:T(8,128)S(1)} %slice.105), channel_id=1, source_target_pairs={{0,32},{1,9},{2,34},{3,11},{4,36},{5,13},{6,38},{7,15},{8,40},{9,1... | collective-permute-start | bytes 1572872 | tf_op jit(solution)/shard_map/ppermute | solution.py:54
  162.8 9.6 %collective-permute-start.30 = (f32[256,512]{1,0:T(8,128)S(1)}, f32[256,512]{1,0:T(8,128)S(1)}, u32[]{:S(2)}, u32[]{:S(2)}) collective-permute-start(f32[256,512]{1,0:T(8,128)S(1)} %slice.106), channel_id=1, source_target_pairs={{0,96},{1,25},{2,98},{3,27},{4,100},{5,29},{6,102},{7,31},{8,104},... | collective-permute-start | bytes 1572872 | tf_op jit(solution)/shard_map/ppermute | solution.py:54
  164.8 8.5 %collective-permute-start.22 = (f32[4,64,512]{2,1,0:T(8,128)S(1)}, f32[4,64,512]{2,1,0:T(8,128)S(1)}, u32[]{:S(2)}, u32[]{:S(2)}) collective-permute-start(f32[4,64,512]{2,1,0:T(8,128)S(1)} %pad_maximum_fusion.2), channel_id=1, source_target_pairs={{0,1},{1,0},{2,3},{3,2},{4,5},{5,4},{6,7},{7,6},{8,9},{9,8},{10,11... | collective-permute-start | bytes 1572872 | tf_op jit(solution)/shard_map/ppermute | solution.py:54
  173.5 56.5 %collective-permute-start.11 = (f32[768,512]{1,0:T(8,128)S(1)}, f32[768,512]{1,0:T(8,128)S(1)}, u32[]{:S(2)}, u32[]{:S(2)}) collective-permute-start(f32[768,512]{1,0:T(8,128)S(1)} %slice.98), channel_id=1, source_target_pairs={{0,32},{1,9},{2,34},{3,11},{4,36},{5,13},{6,38},{7,15},{8,40},{9,1... | collective-permute-start | bytes 4718600 | tf_op jit(solution)/shard_map/ppermute | solution.py:54
  175.6 55.7 %collective-permute-start.12 = (f32[768,512]{1,0:T(8,128)S(1)}, f32[768,512]{1,0:T(8,128)S(1)}, u32[]{:S(2)}, u32[]{:S(2)}) collective-permute-start(f32[768,512]{1,0:T(8,128)S(1)} %slice.99), channel_id=1, source_target_pairs={{0,96},{1,25},{2,98},{3,27},{4,100},{5,29},{6,102},{7,31},{8,104},... | collective-permute-start | bytes 4718600 | tf_op jit(solution)/shard_map/ppermute | solution.py:54
  222.1 7.9 %copy-start.2 = (bf16[4,512,1536]{2,1,0:T(8,128)(2,1)}, bf16[4,512,1536]{2,1,0:T(8,128)(2,1)S(1)}, u32[]{:S(2)}) copy-start(bf16[4,512,1536]{2,1,0:T(8,128)(2,1)S(1)} %get-tuple-element.5.x_ref) | copy-start | bytes 18874372
  222.1 7.9 %copy-start.3 = (bf16[512,1536]{1,0:T(8,128)(2,1)}, bf16[512,1536]{1,0:T(8,128)(2,1)S(1)}, u32[]{:S(2)}) copy-start(bf16[512,1536]{1,0:T(8,128)(2,1)S(1)} %get-tuple-element.7.li_ref) | copy-start | bytes 4718596
  222.1 7.9 %copy-start.4 = (f32[512,512]{1,0:T(8,128)}, f32[512,512]{1,0:T(8,128)S(1)}, u32[]{:S(2)}) copy-start(f32[512,512]{1,0:T(8,128)S(1)} %get-tuple-element.6.l_ref) | copy-start | bytes 3145732
Sparse Core Ops, SparseCore 0:
  41.4 63.7 all-gather.2
